TPU v7x, 32 devices: a whole 2x2x4 slice. The times are simulated.
32 devices in a mesh: row: 4 (over y, core), col: 8 (over z, x).
Axes of the slice: x: 2, y: 2, z: 4, core: 2. Of those that a mesh axis runs over, the one named last changes fastest.
Arguments:
- particles: float32 [1024, 128], P('row'), may hold values from -4 to 4
- log_weights: float32 [1024], P('row'), may hold values from -8 to 8
- targets: float32 [3072, 128], P('col'), may hold values from -5 to 5
Outputs:
- new_particles: float32 [3072, 128], P(('col', 'row'))
All inputs are finite; a program needn't handle non-finite values.
Results may differ from a plain program's by a relative error of at most 0.005.
Values sent between devices are 32-bit elements; how exact they have to be, the bound alone decides.
A program may use at most 64 MiB of HBM per device.

v0:
```python
import math

import jax
import jax.numpy as jnp
from jax import lax
from jax.sharding import PartitionSpec as P

ITERS = 3


EPS = 0.01


def cost_tile(source, points):
    source_sq = jnp.sum(source * source, axis=1)
    points_sq = jnp.sum(points * points, axis=1)
    cross = jnp.dot(
        source, points.T, precision=lax.Precision.HIGHEST, preferred_element_type=jnp.float32
    )
    return (source_sq[:, None] + points_sq[None, :] - 2.0 * cross) / source.shape[1]


def row_update(particles, log_weights, targets, col_pot, block_count, block_rows):
    maxima = []
    totals = []
    for index in range(block_count):
        source = particles[index * block_rows : (index + 1) * block_rows]
        scores = (col_pot[None, :] - cost_tile(source, targets)) / EPS
        top = jnp.max(scores, axis=1)
        maxima.append(top)
        totals.append(jnp.sum(jnp.exp(scores - top[:, None]), axis=1))
    local_top = jnp.concatenate(maxima)
    local_sum = jnp.concatenate(totals)
    top = lax.pmax(local_top, "col")
    summed = lax.psum(local_sum * jnp.exp(local_top - top), "col")
    return EPS * (log_weights - (top + jnp.log(summed)))


def col_update(particles, targets, row_pot, block_count, block_rows):
    width = targets.shape[0]
    top = jnp.full((width,), -1e30, jnp.float32)
    summed = jnp.zeros((width,), jnp.float32)
    for index in range(block_count):
        source = particles[index * block_rows : (index + 1) * block_rows]
        potential = row_pot[index * block_rows : (index + 1) * block_rows]
        scores = (potential[:, None] - cost_tile(source, targets)) / EPS
        fresh = jnp.maximum(top, jnp.max(scores, axis=0))
        summed = summed * jnp.exp(top - fresh) + jnp.sum(jnp.exp(scores - fresh[None, :]), axis=0)
        top = fresh
    global_top = lax.pmax(top, "row")
    summed = lax.psum(summed * jnp.exp(top - global_top), "row")
    top = global_top
    return top + jnp.log(summed)


def per_device(particles, log_weights, targets):
    row_count = particles.shape[0]
    block_count = max(1, row_count // 512)
    block_rows = row_count // block_count
    log_count = math.log(targets.shape[0] * lax.axis_size("col"))
    col_pot = jnp.zeros((targets.shape[0],), jnp.float32)
    col_lse = col_pot
    row_pot = log_weights
    for iteration in range(ITERS):
        row_pot = row_update(particles, log_weights, targets, col_pot, block_count, block_rows)
        col_lse = col_update(particles, targets, row_pot, block_count, block_rows)
        col_pot = EPS * (-log_count - col_lse)
    particles_half = particles.astype(jnp.bfloat16)
    acc = jnp.zeros(
        (lax.axis_size("row") * (targets.shape[0] // lax.axis_size("row")), particles.shape[1]),
        jnp.float32,
    )
    for index in range(block_count):
        source = particles[index * block_rows : (index + 1) * block_rows]
        potential = row_pot[index * block_rows : (index + 1) * block_rows]
        plan = jnp.exp(
            (potential[:, None] - cost_tile(source, targets)) / EPS - col_lse[None, :]
        ).astype(jnp.bfloat16)
        source_half = particles_half[index * block_rows : (index + 1) * block_rows]
        acc = acc + lax.dot_general(
            plan, source_half, (((0,), (0,)), ((), ())), preferred_element_type=jnp.float32
        )
    return lax.psum_scatter(acc, "row", scatter_dimension=0, tiled=True)


def solution(mesh):
    placed = (P("row", None), P("row"), P("col", None))
    return jax.shard_map(
        per_device, mesh=mesh, in_specs=placed, out_specs=P(("col", "row"), None), check_vma=False
    )
```

profile of v0, /device:TPU:0, one launch (start us, length us, event | category | flops | bytes accessed | tf_op | source)
XLA Modules:
  0.0 186.4 jit_solution(17836012105092089794)
XLA Ops:
  6.5 0.0 copy-start.1
  6.5 0.0 reduce-scatter.2.cloned.1.call-start
  6.5 1.1 multiply_reduce_fusion.1
  7.6 0.0 copy-start
  7.6 1.1 multiply_reduce_fusion
  8.7 0.0 copy-done.1
  8.7 0.0 copy-done
  8.7 0.6 fusion.2
  9.4 23.1 %pmax.42 = f32[256]{0:T(256)S(1)} all-reduce(f32[256]{0:T(256)S(1)} %get-tuple-element.5), channel_id=1, replica_groups=mesh['row'=4,'col'=8] {'col'}, use_global_device_ids=true, to_apply=%region_3.0 | all-reduce | flops 256 | bytes 2048 | tf_op jit(solution)/shard_map/pmax | solution.py:34
  32.5 0.2 exponential_reduce_fusion.5
  32.7 0.0 copy-start.2
  32.7 17.1 %psum.42 = f32[256]{0:T(256)S(1)} all-reduce(f32[256]{0:T(256)S(1)} %exponential_multiply_fusion.5), channel_id=1, replica_groups=mesh['row'=4,'col'=8] {'col'}, use_global_device_ids=true, to_apply=%region_5.0 | all-reduce | flops 256 | bytes 2048 | tf_op jit(solution)/shard_map/psum | solution.py:35
  49.8 0.0 copy-done.2
  49.8 0.1 fusion.3
  50.0 0.2 exponential_reduce_fusion.4
  50.1 5.7 %pmax.43 = f32[384]{0:T(512)S(1)} all-reduce(f32[384]{0:T(512)S(1)} %broadcast_maximum_fusion.2), channel_id=1, replica_groups=mesh['row'=4,'col'=8] {'row'}, use_global_device_ids=true, to_apply=%region_7.0 | all-reduce | flops 384 | bytes 3072 | tf_op jit(solution)/shard_map/pmax | solution.py:50
  55.8 6.6 %psum.43 = f32[384]{0:T(512)S(1)} all-reduce(f32[384]{0:T(512)S(1)} %exponential_multiply_fusion.2), channel_id=1, replica_groups=mesh['row'=4,'col'=8] {'row'}, use_global_device_ids=true, to_apply=%region_9.0 | all-reduce | flops 384 | bytes 3072 | tf_op jit(solution)/shard_map/psum | solution.py:51
  62.5 0.1 fusion.4
  62.6 0.2 exponential_reduce_fusion.3
  62.8 19.1 %pmax.44 = f32[256]{0:T(256)S(1)} all-reduce(f32[256]{0:T(256)S(1)} %fusion.4), channel_id=1, replica_groups=mesh['row'=4,'col'=8] {'col'}, use_global_device_ids=true, to_apply=%region_11.0 | all-reduce | flops 256 | bytes 2048 | tf_op jit(solution)/shard_map/pmax | solution.py:34
  82.0 17.1 %psum.44 = f32[256]{0:T(256)S(1)} all-reduce(f32[256]{0:T(256)S(1)} %exponential_multiply_fusion.4), channel_id=1, replica_groups=mesh['row'=4,'col'=8] {'col'}, use_global_device_ids=true, to_apply=%region_13.0 | all-reduce | flops 256 | bytes 2048 | tf_op jit(solution)/shard_map/psum | solution.py:35
  99.1 0.1 fusion.5
  99.2 0.2 exponential_reduce_fusion.2
  99.4 5.7 %pmax.45 = f32[384]{0:T(512)S(1)} all-reduce(f32[384]{0:T(512)S(1)} %broadcast_maximum_fusion.1), channel_id=1, replica_groups=mesh['row'=4,'col'=8] {'row'}, use_global_device_ids=true, to_apply=%region_15.0 | all-reduce | flops 384 | bytes 3072 | tf_op jit(solution)/shard_map/pmax | solution.py:50
  105.1 6.3 %psum.45 = f32[384]{0:T(512)S(1)} all-reduce(f32[384]{0:T(512)S(1)} %exponential_multiply_fusion.1), channel_id=1, replica_groups=mesh['row'=4,'col'=8] {'row'}, use_global_device_ids=true, to_apply=%region_17.0 | all-reduce | flops 384 | bytes 3072 | tf_op jit(solution)/shard_map/psum | solution.py:51
  111.3 0.1 fusion.6
  111.5 0.2 exponential_reduce_fusion.1
  111.7 19.1 %pmax.46 = f32[256]{0:T(256)S(1)} all-reduce(f32[256]{0:T(256)S(1)} %fusion.6), channel_id=1, replica_groups=mesh['row'=4,'col'=8] {'col'}, use_global_device_ids=true, to_apply=%region_19.0 | all-reduce | flops 256 | bytes 2048 | tf_op jit(solution)/shard_map/pmax | solution.py:34
  130.8 17.1 %psum.46 = f32[256]{0:T(256)S(1)} all-reduce(f32[256]{0:T(256)S(1)} %exponential_multiply_fusion.3), channel_id=1, replica_groups=mesh['row'=4,'col'=8] {'col'}, use_global_device_ids=true, to_apply=%region_21.0 | all-reduce | flops 256 | bytes 2048 | tf_op jit(solution)/shard_map/psum | solution.py:35
  148.0 0.1 fusion.7
  148.1 5.7 %pmax.47 = f32[384]{0:T(512)S(1)} all-reduce(f32[384]{0:T(512)S(1)} %broadcast_maximum_fusion), channel_id=1, replica_groups=mesh['row'=4,'col'=8] {'row'}, use_global_device_ids=true, to_apply=%region_23.0 | all-reduce | flops 384 | bytes 3072 | tf_op jit(solution)/shard_map/pmax | solution.py:50
  153.8 0.2 exponential_reduce_fusion
  154.0 6.5 %psum.47 = f32[384]{0:T(512)S(1)} all-reduce(f32[384]{0:T(512)S(1)} %exponential_multiply_fusion), channel_id=1, replica_groups=mesh['row'=4,'col'=8] {'row'}, use_global_device_ids=true, to_apply=%region_25.0 | all-reduce | flops 384 | bytes 3072 | tf_op jit(solution)/shard_map/psum | solution.py:51
  160.5 1.0 fusion.8
  161.5 0.0 reduce-scatter.2.cloned.1.call-update
  161.5 18.0 %reduce-scatter.2.cloned.1.call-done = f32[96,128]{1,0:T(8,128)} async-done(((f32[384,128]{1,0:T(8,128)}), f32[96,128]{1,0:T(8,128)}) %reduce-scatter.2.cloned.1.call-update) | async-done | bytes 49168 | tf_op jit(solution)/shard_map/reduce_scatter | solution.py:83
  (15 shorter events, 0.1 us)
Async XLA Ops:
  6.5 2.2 %copy-start.1 = (f32[384,128]{1,0:T(8,128)S(1)}, f32[384,128]{1,0:T(8,128)}, u32[]{:S(2)}) copy-start(f32[384,128]{1,0:T(8,128)} %param.5) | copy-start | bytes 589828
  6.5 173.0 %reduce-scatter.2.cloned.1.call-start = ((), (), s32[]{:S(2)}) async-start(), calls=%async_computation.1 | async-start | bytes 245760 | tf_op jit(solution)/shard_map/reduce_scatter | solution.py:83
  7.6 1.1 copy-start
  32.7 17.1 %copy-start.2 = (f32[256]{0:T(256)S(1)}, f32[256]{0:T(256)}, u32[]{:S(2)}) copy-start(f32[256]{0:T(256)} %param.4) | copy-start | bytes 3076
Sparse Core Ops, SparseCore 0:
  161.7 17.8 reduce-scatter.1
where the time goes:
time: 187 us; the launch traced here: 186 us
  blocking collectives  149 us (80%)
  waiting for transfers between devices  18 us (10%)
  between operations  13.5 us (7%)
  other arithmetic  4.04 us (2%)
    pmax x3, blocking collectives, row_update(): top = lax.pmax(local_top, 'col')  61.4 us
    psum x3, blocking collectives, row_update(): summed = lax.psum(local_sum * jnp.exp(local_top - top), 'col')  51.4 us
    psum x3, blocking collectives, col_update(): summed = lax.psum(summed * jnp.exp(top - global_top), 'row')  19.4 us
    reduce_scatter x1, waiting for transfers between devices, per_device(): return lax.psum_scatter(acc, 'row', scatter_dimension=0, tiled=True)  18 us
    pmax x3, blocking collectives, col_update(): global_top = lax.pmax(top, 'row')  17 us
  transfers between devices with their start and end apart: 1, of which 1 were waited for; matrix products, arithmetic and copies ran while one was open for 0% of the time, Pallas kernels for 0%

commit v1 on v0

--- a/solution.py
+++ b/solution.py
@@ -1,22 +1,28 @@
+import functools
 import math
 
 import jax
 import jax.numpy as jnp
 from jax import lax
+from jax.experimental import pallas as pl
+from jax.experimental.pallas import tpu as pltpu
 from jax.sharding import PartitionSpec as P
 
 ITERS = 3
 
 
 EPS = 0.01
+MESH = pl.DeviceIdType.MESH
+HIGHEST = lax.Precision.HIGHEST
+LANES = 128
+CHUNK = 32
+PIECES = 2
 
 
 def cost_tile(source, points):
     source_sq = jnp.sum(source * source, axis=1)
     points_sq = jnp.sum(points * points, axis=1)
-    cross = jnp.dot(
-        source, points.T, precision=lax.Precision.HIGHEST, preferred_element_type=jnp.float32
-    )
+    cross = jnp.dot(source, points.T, precision=HIGHEST, preferred_element_type=jnp.float32)
     return (source_sq[:, None] + points_sq[None, :] - 2.0 * cross) / source.shape[1]
 
 
@@ -49,11 +55,10 @@
         top = fresh
     global_top = lax.pmax(top, "row")
     summed = lax.psum(summed * jnp.exp(top - global_top), "row")
-    top = global_top
-    return top + jnp.log(summed)
-
-
-def per_device(particles, log_weights, targets):
+    return global_top + jnp.log(summed)
+
+
+def per_device_large(particles, log_weights, targets):
     row_count = particles.shape[0]
     block_count = max(1, row_count // 512)
     block_rows = row_count // block_count
@@ -83,8 +88,262 @@
     return lax.psum_scatter(acc, "row", scatter_dimension=0, tiled=True)
 
 
+def dot_minor(a, b, precision):
+    return lax.dot_general(
+        a, b, (((1,), (1,)), ((), ())), precision=precision, preferred_element_type=jnp.float32
+    )
+
+
+def kernel(
+    cols,
+    x_hbm,
+    w_ref,
+    y_hbm,
+    out_ref,
+    held,
+    points,
+    tile,
+    sums,
+    part1,
+    part2,
+    part3,
+    pots,
+    local_sem,
+    pair_sem,
+    far_sem,
+    fwd_sem,
+    pot_sem,
+    part_sem,
+):
+    rows = 4
+    row = lax.axis_index("row")
+    col = lax.axis_index("col")
+    side = lax.rem(row, 2)
+    twin = row + 1 - 2 * side
+    far = lax.rem(row + 2, rows)
+    far_twin = lax.rem(twin + 2, rows)
+    block, feature = x_hbm.shape
+    width = y_hbm.shape[0]
+    total = rows * block
+    groups = block // LANES
+    piece = block // PIECES
+
+    load_x = pltpu.make_async_copy(x_hbm, held.at[0], local_sem.at[0])
+    load_y = pltpu.make_async_copy(y_hbm, points, local_sem.at[1])
+    load_x.start()
+    load_y.start()
+
+    barrier = pltpu.get_barrier_semaphore()
+    for peer in (twin, far, far_twin):
+        pl.semaphore_signal(barrier, inc=1, device_id=(peer, col), device_id_type=MESH)
+    for step in range(1, cols):
+        pl.semaphore_signal(
+            barrier, inc=1, device_id=(row, lax.rem(col + step, cols)), device_id_type=MESH
+        )
+    load_x.wait()
+    load_y.wait()
+    pl.semaphore_wait(barrier, rows - 1 + cols - 1)
+
+    def send(src, dst, sems, index, device):
+        copy = pltpu.make_async_remote_copy(
+            src_ref=src,
+            dst_ref=dst,
+            send_sem=sems.at[0, index],
+            recv_sem=sems.at[1, index],
+            device_id=device,
+            device_id_type=MESH,
+        )
+        copy.start()
+        return copy
+
+    sent = []
+    far_copies = []
+    for index in range(PIECES):
+        span = pl.ds(index * piece, piece)
+        far_copies.append(
+            send(held.at[0, span], held.at[2, span], far_sem, index, (far, col))
+        )
+    pair_copy = send(held.at[0], held.at[1], pair_sem, 0, (twin, col))
+
+    scale = 2.0 / (feature * EPS)
+    half = 1.0 / (feature * EPS)
+
+    def score(slot):
+        source = held[slot]
+        square = dot_minor(jnp.ones((8, feature), jnp.float32), source * source, HIGHEST)[:1]
+        y = points[...]
+        y_square = jnp.sum(y * y, axis=1, keepdims=True)
+        cross = dot_minor(y * scale, source, HIGHEST)
+        tile[:, slot * block : (slot + 1) * block] = cross - (y_square + square) * half
+
+    def exchange(part, index):
+        copies = []
+        for step in range(1, cols):
+            copies.append(
+                send(
+                    part.at[0],
+                    part.at[step],
+                    part_sem.at[index],
+                    step,
+                    (row, lax.rem(col + step, cols)),
+                )
+            )
+        return copies
+
+    score(0)
+    own = tile[:, :block]
+    top = jnp.max(own, axis=0, keepdims=True)
+    lse = top + jnp.log(jnp.sum(jnp.exp(own - top), axis=0, keepdims=True))
+    for group in range(groups):
+        part1[0, group : group + 1, :] = lse[:, group * LANES : (group + 1) * LANES]
+    first = exchange(part1, 0)
+
+    pair_copy.wait_recv()
+    score(1)
+    forwards = []
+    for index in range(PIECES):
+        if index == PIECES - 1:
+            for copy in first:
+                copy.wait_recv()
+            every = part1[:, :groups, :]
+            top = jnp.max(every, axis=0)
+            row_lse = top + jnp.log(jnp.sum(jnp.exp(every - top[None]), axis=0))
+            weights = w_ref[...]
+            pots[0, :groups, :] = weights - row_lse
+            pots[0, groups : 2 * groups, :] = weights
+            pot_copies = [
+                send(pots.at[0], pots.at[slot], pot_sem, slot, (peer, col))
+                for slot, peer in ((1, twin), (2, far), (3, far_twin))
+            ]
+        far_copies[index].wait_recv()
+        span = pl.ds(index * piece, piece)
+        forwards.append(send(held.at[2, span], held.at[3, span], fwd_sem, index, (twin, col)))
+    score(2)
+    for copy in forwards:
+        copy.wait_recv()
+    score(3)
+    for copy in pot_copies:
+        copy.wait_recv()
+
+    def spread(compact):
+        return jnp.concatenate([compact[g : g + 1, :] for g in range(rows * groups)], axis=1)
+
+    def gathered(first_row):
+        return jnp.concatenate(
+            [pots[slot, first_row : first_row + groups, :] for slot in range(rows)], axis=0
+        )
+
+    row_pot = spread(gathered(0))
+    mass = jnp.exp(gathered(groups)) * float(width * cols)
+
+    chunks = [slice(c * CHUNK, (c + 1) * CHUNK) for c in range(width // CHUNK)]
+
+    for rows_of in chunks:
+        shifted = tile[rows_of, :] + row_pot
+        tile[rows_of, :] = shifted
+        fold = shifted[:, :LANES]
+        for g in range(1, rows * groups):
+            fold = jnp.maximum(fold, shifted[:, g * LANES : (g + 1) * LANES])
+        sums[rows_of, :] = fold
+    tops = jnp.max(sums[...], axis=1, keepdims=True)
+    for index, rows_of in enumerate(chunks):
+        entries = jnp.exp(tile[rows_of, :] - tops[rows_of])
+        tile[rows_of, :] = entries
+        fold = entries[:, :LANES]
+        for g in range(1, rows * groups):
+            fold = fold + entries[:, g * LANES : (g + 1) * LANES]
+        sums[rows_of, :] = fold
+    inverse = 1.0 / jnp.sum(sums[...], axis=1, keepdims=True)
+
+    def row_sums(inverse, part):
+        acc = jnp.zeros((8, total), jnp.float32)
+        for rows_of in chunks:
+            scaled = tile[rows_of, :] * inverse[rows_of]
+            acc = acc + jnp.sum(scaled.reshape(CHUNK // 8, 8, total), axis=0)
+        summed = jnp.sum(acc, axis=0, keepdims=True)
+        for g in range(rows * groups):
+            part[0, g : g + 1, :] = summed[:, g * LANES : (g + 1) * LANES]
+
+    def finish(copies, part):
+        for copy in copies:
+            copy.wait_recv()
+        return spread(mass / jnp.sum(part[...], axis=0))
+
+    row_sums(inverse, part2)
+    second = exchange(part2, 1)
+    factor = finish(second, part2)
+
+    for rows_of in chunks:
+        fold = jnp.zeros((CHUNK, LANES), jnp.float32)
+        for g in range(rows * groups):
+            lanes = slice(g * LANES, (g + 1) * LANES)
+            fold = fold + tile[rows_of, lanes] * factor[:, lanes]
+        sums[rows_of, :] = fold
+    inverse = 1.0 / jnp.sum(sums[...], axis=1, keepdims=True)
+    row_sums(inverse, part3)
+    third = exchange(part3, 2)
+    source_half = held[...].reshape(total, feature).astype(jnp.bfloat16)
+    factor = finish(third, part3)
+
+    share = width // rows
+    mine = tile[pl.ds(pl.multiple_of(row * share, 8), share), :] * factor
+    plan = mine * (1.0 / jnp.sum(mine, axis=1, keepdims=True))
+    out_ref[...] = jnp.dot(
+        plan.astype(jnp.bfloat16), source_half, preferred_element_type=jnp.float32
+    )
+
+    for copy in far_copies + [pair_copy] + forwards + pot_copies + first + second + third:
+        copy.wait_send()
+
+
+def per_device_small(cols, particles, log_weights, targets):
+    block, feature = particles.shape
+    width = targets.shape[0]
+    groups = block // LANES
+    part = pltpu.VMEM((cols, 8, LANES), jnp.float32)
+    any_space = pl.BlockSpec(memory_space=pl.ANY)
+    vmem = pl.BlockSpec(memory_space=pltpu.VMEM)
+    return pl.pallas_call(
+        functools.partial(kernel, cols),
+        out_shape=jax.ShapeDtypeStruct((width // 4, feature), jnp.float32),
+        in_specs=[any_space, vmem, any_space],
+        out_specs=vmem,
+        scratch_shapes=[
+            pltpu.VMEM((4, block, feature), jnp.float32),
+            pltpu.VMEM((width, feature), jnp.float32),
+            pltpu.VMEM((width, 4 * block), jnp.float32),
+            pltpu.VMEM((width, LANES), jnp.float32),
+            part,
+            part,
+            part,
+            pltpu.VMEM((4, 8, LANES), jnp.float32),
+            pltpu.SemaphoreType.DMA((2,)),
+            pltpu.SemaphoreType.DMA((2, 1)),
+            pltpu.SemaphoreType.DMA((2, PIECES)),
+            pltpu.SemaphoreType.DMA((2, PIECES)),
+            pltpu.SemaphoreType.DMA((2, 4)),
+            pltpu.SemaphoreType.DMA((3, 2, cols)),
+        ],
+        compiler_params=pltpu.CompilerParams(
+            collective_id=0, has_side_effects=True, vmem_limit_bytes=32 * 1024 * 1024
+        ),
+    )(particles, log_weights.reshape(groups, LANES), targets)
+
+
+def per_device(rows, cols, particles, log_weights, targets):
+    block = particles.shape[0]
+    width = targets.shape[0]
+    if rows == 4 and block == 2 * LANES and width % (4 * CHUNK) == 0 and width <= 2048:
+        return per_device_small(cols, particles, log_weights, targets)
+    return per_device_large(particles, log_weights, targets)
+
+
 def solution(mesh):
     placed = (P("row", None), P("row"), P("col", None))
     return jax.shard_map(
-        per_device, mesh=mesh, in_specs=placed, out_specs=P(("col", "row"), None), check_vma=False
+        functools.partial(per_device, mesh.shape["row"], mesh.shape["col"]),
+        mesh=mesh,
+        in_specs=placed,
+        out_specs=P(("col", "row"), None),
+        check_vma=False,
     )

time: 187 us -> 26.2 us (0.14)
  blocking collectives: 149 us -> 0 us
  Pallas kernels: 0 us -> 22.9 us
  waiting for transfers between devices: 18 us -> 0 us
  between operations: 13.5 us -> 0.01 us
  other arithmetic: 4.04 us -> 0 us
  local copies, waits for them, and re-layouts: 0.02 us -> 3.13 us
    pmax x6 -> x0, blocking collectives: 78.4 us -> none  [the longest x3 61.4 us: row_update(): top = lax.pmax(local_top, 'col')]
    psum x6 -> x0, blocking collectives: 70.8 us -> none  [the longest x3 51.4 us: row_update(): summed = lax.psum(local_sum * jnp.exp(local_top - top), 'col')]
    pallas_call x0 -> x1, Pallas kernels: none -> 22.9 us  [per_device_small(): pl.pallas_call(functools.partial(kernel, cols), out_shape=jax.ShapeDtypeS...]
    reduce_scatter x1 -> x0, waiting for transfers between devices: 18 us -> none  [per_device(): return lax.psum_scatter(acc, 'row', scatter_dimension=0, tiled=True)]
    reduce_sum x8 -> x0, other arithmetic: 3.28 us -> none  [the longest x1 1.11 us: cost_tile(): points_sq = jnp.sum(points * points, axis=1)]
    unnamed x6 -> x7, local copies, waits for them, and re-layouts: 0.02 us -> 3.13 us
  transfers between devices with their start and end apart: 1 -> 0, of which waited for: 1 -> 0; matrix products, arithmetic and copies ran while one was open for 0% -> 0% of each run, Pallas kernels for 0% -> 0%
where the time goes in v1:
time: 26.2 us; the launch traced here: 26 us
  Pallas kernels  22.9 us (87%)
  local copies, waits for them, and re-layouts  3.13 us (12%)
    pallas_call x1, Pallas kernels, per_device_small(): pl.pallas_call(functools.partial(kernel, cols), out_shape=jax.ShapeDtypeS...  22.9 us
    unnamed x7, local copies, waits for them, and re-layouts  3.13 us

profile of v1, /device:TPU:0, one launch (start us, length us, event | category | flops | bytes accessed | tf_op | source)
XLA Modules:
  0.0 26.0 jit_solution(15635538544385007541)
XLA Ops:
  0.0 0.0 copy-start.2
  0.0 0.7 %copy-done.2 = f32[256]{0:T(256)S(1)} copy-done((f32[256]{0:T(256)S(1)}, f32[256]{0:T(256)}, u32[]{:S(2)}) %copy-start.2) | copy-done | bytes 1048
  0.7 0.0 copy-start
  0.7 0.9 %copy-done = f32[384,128]{1,0:T(8,128)S(1)} copy-done((f32[384,128]{1,0:T(8,128)S(1)}, f32[384,128]{1,0:T(8,128)}, u32[]{:S(2)}) %copy-start) | copy-done | bytes 196632
  1.6 0.0 copy-start.1
  1.6 0.9 %copy-done.1 = f32[256,128]{1,0:T(8,128)S(1)} copy-done((f32[256,128]{1,0:T(8,128)S(1)}, f32[256,128]{1,0:T(8,128)}, u32[]{:S(2)}) %copy-start.1) | copy-done | bytes 131096
  2.5 22.9 %shard_map.37 = f32[96,128]{1,0:T(8,128)S(1)} custom-call(f32[256,128]{1,0:T(8,128)S(1)} %copy-done.1, f32[2,128]{1,0:T(2,128)S(1)} %bitcast.1, f32[384,128]{1,0:T(8,128)S(1)} %copy-done), custom_call_target="tpu_custom_call" | custom-call | tf_op jit(solution)/shard_map/pallas_call | solution.py:306
  25.4 0.6 %copy.5 = f32[96,128]{1,0:T(8,128)} copy(f32[96,128]{1,0:T(8,128)S(1)} %shard_map.37) | data formatting | bytes 98304
Async XLA Ops:
  0.0 0.7 %copy-start.2 = (f32[256]{0:T(256)S(1)}, f32[256]{0:T(256)}, u32[]{:S(2)}) copy-start(f32[256]{0:T(256)} %param.4) | copy-start | bytes 3076
  0.7 0.9 %copy-start = (f32[384,128]{1,0:T(8,128)S(1)}, f32[384,128]{1,0:T(8,128)}, u32[]{:S(2)}) copy-start(f32[384,128]{1,0:T(8,128)} %y_hbm.1) | copy-start | bytes 589828
  1.6 0.9 %copy-start.1 = (f32[256,128]{1,0:T(8,128)S(1)}, f32[256,128]{1,0:T(8,128)}, u32[]{:S(2)}) copy-start(f32[256,128]{1,0:T(8,128)} %x_hbm.1) | copy-start | bytes 393220

commit v2 on v1

--- a/solution.py
+++ b/solution.py
@@ -94,14 +94,25 @@
     )
 
 
+def split(values):
+    high = values.astype(jnp.bfloat16)
+    rest = values - high.astype(jnp.float32)
+    middle = rest.astype(jnp.bfloat16)
+    low = (rest - middle.astype(jnp.float32)).astype(jnp.bfloat16)
+    return high, middle, low
+
+
 def kernel(
     cols,
     x_hbm,
-    w_ref,
+    w_hbm,
     y_hbm,
     out_ref,
     held,
     points,
+    weights_ref,
+    point_parts,
+    source_half,
     tile,
     sums,
     part1,
@@ -130,8 +141,10 @@
 
     load_x = pltpu.make_async_copy(x_hbm, held.at[0], local_sem.at[0])
     load_y = pltpu.make_async_copy(y_hbm, points, local_sem.at[1])
+    load_w = pltpu.make_async_copy(w_hbm, weights_ref, local_sem.at[2])
+    load_y.start()
     load_x.start()
-    load_y.start()
+    load_w.start()
 
     barrier = pltpu.get_barrier_semaphore()
     for peer in (twin, far, far_twin):
@@ -140,9 +153,6 @@
         pl.semaphore_signal(
             barrier, inc=1, device_id=(row, lax.rem(col + step, cols)), device_id_type=MESH
         )
-    load_x.wait()
-    load_y.wait()
-    pl.semaphore_wait(barrier, rows - 1 + cols - 1)
 
     def send(src, dst, sems, index, device):
         copy = pltpu.make_async_remote_copy(
@@ -156,25 +166,21 @@
         copy.start()
         return copy
 
-    sent = []
-    far_copies = []
-    for index in range(PIECES):
-        span = pl.ds(index * piece, piece)
-        far_copies.append(
-            send(held.at[0, span], held.at[2, span], far_sem, index, (far, col))
-        )
-    pair_copy = send(held.at[0], held.at[1], pair_sem, 0, (twin, col))
-
     scale = 2.0 / (feature * EPS)
     half = 1.0 / (feature * EPS)
+    load_y.wait()
+    y = points[...]
+    y_square = jnp.sum(y * y, axis=1, keepdims=True) * half
+    high, middle, low = split(y * scale)
+    for place, part in enumerate((high, middle, high, middle, high, low)):
+        point_parts[:, place * feature : (place + 1) * feature] = part
 
     def score(slot):
-        source = held[slot]
-        square = dot_minor(jnp.ones((8, feature), jnp.float32), source * source, HIGHEST)[:1]
-        y = points[...]
-        y_square = jnp.sum(y * y, axis=1, keepdims=True)
-        cross = dot_minor(y * scale, source, HIGHEST)
-        tile[:, slot * block : (slot + 1) * block] = cross - (y_square + square) * half
+        high, middle, low = split(held[slot])
+        source_half[slot * block : (slot + 1) * block, :] = high
+        source_parts = jnp.concatenate([high, high, middle, middle, low, high], axis=1)
+        cross = dot_minor(point_parts[...], source_parts, None)
+        tile[:, slot * block : (slot + 1) * block] = cross - y_square
 
     def exchange(part, index):
         copies = []
@@ -190,13 +196,27 @@
             )
         return copies
 
+    load_x.wait()
+    load_w.wait()
     score(0)
-    own = tile[:, :block]
+    source = held[0]
+    square = dot_minor(jnp.ones((8, feature), jnp.float32), source * source, HIGHEST)[:1] * half
+    own = tile[:, :block] - square
     top = jnp.max(own, axis=0, keepdims=True)
     lse = top + jnp.log(jnp.sum(jnp.exp(own - top), axis=0, keepdims=True))
     for group in range(groups):
         part1[0, group : group + 1, :] = lse[:, group * LANES : (group + 1) * LANES]
+
+    pl.semaphore_wait(barrier, rows - 1 + cols - 1)
+
     first = exchange(part1, 0)
+    far_copies = []
+    for index in range(PIECES):
+        span = pl.ds(index * piece, piece)
+        far_copies.append(
+            send(held.at[0, span], held.at[2, span], far_sem, index, (far, col))
+        )
+    pair_copy = send(held.at[0], held.at[1], pair_sem, 0, (twin, col))
 
     pair_copy.wait_recv()
     score(1)
@@ -208,8 +228,11 @@
             every = part1[:, :groups, :]
             top = jnp.max(every, axis=0)
             row_lse = top + jnp.log(jnp.sum(jnp.exp(every - top[None]), axis=0))
-            weights = w_ref[...]
-            pots[0, :groups, :] = weights - row_lse
+            weights = weights_ref[...]
+            for group in range(groups):
+                pots[0, group : group + 1, :] = (weights - row_lse)[group : group + 1] - square[
+                    :, group * LANES : (group + 1) * LANES
+                ]
             pots[0, groups : 2 * groups, :] = weights
             pot_copies = [
                 send(pots.at[0], pots.at[slot], pot_sem, slot, (peer, col))
@@ -240,14 +263,13 @@
 
     for rows_of in chunks:
         shifted = tile[rows_of, :] + row_pot
-        tile[rows_of, :] = shifted
         fold = shifted[:, :LANES]
         for g in range(1, rows * groups):
             fold = jnp.maximum(fold, shifted[:, g * LANES : (g + 1) * LANES])
         sums[rows_of, :] = fold
     tops = jnp.max(sums[...], axis=1, keepdims=True)
     for index, rows_of in enumerate(chunks):
-        entries = jnp.exp(tile[rows_of, :] - tops[rows_of])
+        entries = jnp.exp((tile[rows_of, :] + row_pot) - tops[rows_of])
         tile[rows_of, :] = entries
         fold = entries[:, :LANES]
         for g in range(1, rows * groups):
@@ -282,14 +304,13 @@
     inverse = 1.0 / jnp.sum(sums[...], axis=1, keepdims=True)
     row_sums(inverse, part3)
     third = exchange(part3, 2)
-    source_half = held[...].reshape(total, feature).astype(jnp.bfloat16)
     factor = finish(third, part3)
 
     share = width // rows
     mine = tile[pl.ds(pl.multiple_of(row * share, 8), share), :] * factor
     plan = mine * (1.0 / jnp.sum(mine, axis=1, keepdims=True))
     out_ref[...] = jnp.dot(
-        plan.astype(jnp.bfloat16), source_half, preferred_element_type=jnp.float32
+        plan.astype(jnp.bfloat16), source_half[...], preferred_element_type=jnp.float32
     )
 
     for copy in far_copies + [pair_copy] + forwards + pot_copies + first + second + third:
@@ -301,23 +322,26 @@
     width = targets.shape[0]
     groups = block // LANES
     part = pltpu.VMEM((cols, 8, LANES), jnp.float32)
-    any_space = pl.BlockSpec(memory_space=pl.ANY)
+    hbm = pl.BlockSpec(memory_space=pltpu.HBM)
     vmem = pl.BlockSpec(memory_space=pltpu.VMEM)
     return pl.pallas_call(
         functools.partial(kernel, cols),
         out_shape=jax.ShapeDtypeStruct((width // 4, feature), jnp.float32),
-        in_specs=[any_space, vmem, any_space],
+        in_specs=[hbm, hbm, hbm],
         out_specs=vmem,
         scratch_shapes=[
             pltpu.VMEM((4, block, feature), jnp.float32),
             pltpu.VMEM((width, feature), jnp.float32),
+            pltpu.VMEM((groups, LANES), jnp.float32),
+            pltpu.VMEM((width, 6 * feature), jnp.bfloat16),
+            pltpu.VMEM((4 * block, feature), jnp.bfloat16),
             pltpu.VMEM((width, 4 * block), jnp.float32),
             pltpu.VMEM((width, LANES), jnp.float32),
             part,
             part,
             part,
             pltpu.VMEM((4, 8, LANES), jnp.float32),
-            pltpu.SemaphoreType.DMA((2,)),
+            pltpu.SemaphoreType.DMA((3,)),
             pltpu.SemaphoreType.DMA((2, 1)),
             pltpu.SemaphoreType.DMA((2, PIECES)),
             pltpu.SemaphoreType.DMA((2, PIECES)),

time: 26.2 us -> 25.7 us (0.981)
  Pallas kernels: 22.9 us -> 22.4 us
    pallas_call x1, Pallas kernels: 22.9 us -> 22.4 us  [per_device_small(): pl.pallas_call(functools.partial(kernel, cols), out_shape=jax.ShapeDtypeS...]
where the time goes in v2:
time: 25.7 us; the launch traced here: 25.5 us
  Pallas kernels  22.4 us (87%)
  local copies, waits for them, and re-layouts  3.13 us (12%)
    pallas_call x1, Pallas kernels, per_device_small(): pl.pallas_call(functools.partial(kernel, cols), out_shape=jax.ShapeDtypeS...  22.4 us
    unnamed x7, local copies, waits for them, and re-layouts  3.13 us

profile of v2, /device:TPU:0, one launch (start us, length us, event | category | flops | bytes accessed | tf_op | source)
XLA Modules:
  0.0 25.5 jit_solution(11833762058634113669)
XLA Ops:
  0.0 0.0 copy-start.2
  0.0 0.7 %copy-done.2 = f32[256]{0:T(256)S(1)} copy-done((f32[256]{0:T(256)S(1)}, f32[256]{0:T(256)}, u32[]{:S(2)}) %copy-start.2) | copy-done | bytes 1048
  0.7 0.0 copy-start
  0.7 0.9 %copy-done = f32[384,128]{1,0:T(8,128)S(1)} copy-done((f32[384,128]{1,0:T(8,128)S(1)}, f32[384,128]{1,0:T(8,128)}, u32[]{:S(2)}) %copy-start) | copy-done | bytes 196632
  1.6 0.0 copy-start.1
  1.6 0.9 %copy-done.1 = f32[256,128]{1,0:T(8,128)S(1)} copy-done((f32[256,128]{1,0:T(8,128)S(1)}, f32[256,128]{1,0:T(8,128)}, u32[]{:S(2)}) %copy-start.1) | copy-done | bytes 131096
  2.5 22.4 %shard_map.37 = f32[96,128]{1,0:T(8,128)S(1)} custom-call(f32[256,128]{1,0:T(8,128)S(1)} %copy-done.1, f32[2,128]{1,0:T(2,128)S(1)} %bitcast.1, f32[384,128]{1,0:T(8,128)S(1)} %copy-done), custom_call_target="tpu_custom_call" | custom-call | tf_op jit(solution)/shard_map/pallas_call | solution.py:327
  24.9 0.6 %copy.5 = f32[96,128]{1,0:T(8,128)} copy(f32[96,128]{1,0:T(8,128)S(1)} %shard_map.37) | data formatting | bytes 98304
Async XLA Ops:
  0.0 0.7 %copy-start.2 = (f32[256]{0:T(256)S(1)}, f32[256]{0:T(256)}, u32[]{:S(2)}) copy-start(f32[256]{0:T(256)} %param.4) | copy-start | bytes 3076
  0.7 0.9 %copy-start = (f32[384,128]{1,0:T(8,128)S(1)}, f32[384,128]{1,0:T(8,128)}, u32[]{:S(2)}) copy-start(f32[384,128]{1,0:T(8,128)} %y_hbm.1) | copy-start | bytes 589828
  1.6 0.9 %copy-start.1 = (f32[256,128]{1,0:T(8,128)S(1)}, f32[256,128]{1,0:T(8,128)}, u32[]{:S(2)}) copy-start(f32[256,128]{1,0:T(8,128)} %x_hbm.1) | copy-start | bytes 393220
